TPU v7x, 32 devices: a whole 2x2x4 slice. The times are simulated.
32 devices in a mesh: cache: 8 (over y, x, core), head: 4 (over z).
Axes of the slice: x: 2, y: 2, z: 4, core: 2. Of those that a mesh axis runs over, the one named last changes fastest.
Arguments:
- tokens: bfloat16 [6144, 8192], P('cache'), may hold values from -6 to 6
- w_x: bfloat16 [8192, 8192], P('cache', 'head'), may hold values from -0.0625 to 0.0625
- w_bc: bfloat16 [8192, 8, 512], P('cache', 'head'), may hold values from -1 to 1
- w_dt: bfloat16 [8192, 128], P('cache', 'head'), may hold values from -0.0625 to 0.0625
- dt_bias: float32 [128], P('head'), may hold values from -3 to -1
- decay_log: float32 [128], P('head'), may hold values from -6.2 to -0.8
- skip_gain: float32 [128], P('head'), may hold values from 0.5 to 1.5
- pool: bfloat16 [64, 256, 8192], P('cache', 'head'), may hold values from -6 to 6
- owners: int32 [48, 1], replicated, may hold values from 0 to 7, as said below
- slots: int32 [48, 1], replicated, may hold values from 0 to 7
- offsets: int32 [48], P('cache'), may hold values from 0 to 31
Outputs:
- mixed: bfloat16 [6144, 8192], P('cache', 'head')
- final_state: bfloat16 [48, 256, 8192], P('cache', None, 'head')
Inputs may be any that keep to these rules, and one draw needn't show every extreme that they name: `owners`: within the 6 rows of one index of cache no two requests name the same owner; every owner is named by some request. `slots`: every slot is named by some request.
All inputs are finite; a program needn't handle non-finite values.
Results may differ from a plain program's by a relative error of at most 0.0039.
Values may be sent and summed in bfloat16 or wider, within the bound.
A program may use at most 256 MiB of HBM per device.

v0:
```python
import jax
import jax.numpy as jnp
from jax import lax
from jax.sharding import PartitionSpec as P

SUFFIX = 128


def body(tokens, w_x, w_bc, w_dt, dt_bias, decay_log, skip_gain, pool, owners, slots, offsets):
    token_count = tokens.shape[0]
    requests_here = token_count // SUFFIX
    heads_here = dt_bias.shape[0]
    groups_here = w_bc.shape[1]
    per_group = heads_here // groups_here
    head_width = w_x.shape[1] // heads_here
    state_size = w_bc.shape[2] // 2
    pieces = (
        lax.all_gather(w_x, "cache", axis=0, tiled=True),
        lax.all_gather(w_bc, "cache", axis=0, tiled=True),
        lax.all_gather(w_dt, "cache", axis=0, tiled=True),
    )
    row_count = pieces[0].shape[0]
    part_x = jnp.dot(tokens, pieces[0], preferred_element_type=jnp.float32)
    part_bc = jnp.dot(tokens, pieces[1].reshape(row_count, -1), preferred_element_type=jnp.float32)
    part_dt = jnp.dot(tokens, pieces[2], preferred_element_type=jnp.float32)
    dt_raw = part_dt
    cache_count = lax.axis_size("cache")
    head_count = lax.axis_size("head")
    my_cache = lax.axis_index("cache")
    owner_table = owners[:, 0].reshape(cache_count, requests_here)
    slot_table = slots[:, 0].reshape(cache_count, requests_here)
    matched = owner_table == my_cache
    chosen_slot = jnp.sum(jnp.where(matched, slot_table, 0), axis=1)
    present = jnp.any(matched, axis=1)
    tiles = jnp.take(pool, chosen_slot, axis=0)
    tiles = jnp.where(present[:, None, None], tiles, jnp.zeros_like(tiles))
    my_owners = lax.dynamic_slice_in_dim(owners[:, 0], my_cache * requests_here, requests_here)
    block_rows = pool.shape[1]
    block_cols = pool.shape[2] // head_count
    blocks = tiles.reshape(cache_count, block_rows, head_count, block_cols)
    received = lax.all_to_all(
        lax.all_to_all(blocks, "cache", split_axis=0, concat_axis=0, tiled=True),
        "head",
        split_axis=2,
        concat_axis=1,
        tiled=True,
    )
    received = received.reshape(cache_count, block_rows * head_count, block_cols)
    start_state = jnp.take(received, my_owners, axis=0)
    chan = part_x.astype(jnp.bfloat16).reshape(requests_here, SUFFIX, heads_here, head_width)
    proj_bc = part_bc.astype(jnp.bfloat16).reshape(
        requests_here, SUFFIX, groups_here, 2 * state_size
    )
    b_part = proj_bc[:, :, :, :state_size]
    c_part = proj_bc[:, :, :, state_size:]
    dt_raw = dt_raw.reshape(requests_here, SUFFIX, heads_here)
    positions = jnp.arange(SUFFIX, dtype=jnp.int32)
    live = (positions[None, :] >= offsets[:, None]).astype(jnp.float32)
    step = jax.nn.softplus(dt_raw + dt_bias[None, None, :]) * live[:, :, None]
    rate = -jnp.exp(decay_log)[None, None, :] * step
    cum = jnp.cumsum(rate, axis=1)
    scores = jnp.einsum("rtgn,rsgn->rgts", c_part, b_part, preferred_element_type=jnp.float32)
    cum_heads = jnp.transpose(cum, (0, 2, 1))
    causal = positions[:, None] >= positions[None, :]
    spread = cum_heads[:, :, :, None] - cum_heads[:, :, None, :]
    decay = jnp.where(causal[None, None], jnp.exp(jnp.where(causal[None, None], spread, 0.0)), 0.0)
    step_heads = jnp.transpose(step, (0, 2, 1))
    decay = decay * step_heads[:, :, None, :]
    decay = decay.reshape(requests_here, groups_here, per_group, SUFFIX, SUFFIX)
    weight = (
        (scores[:, :, None] * decay)
        .astype(jnp.bfloat16)
        .reshape(requests_here, heads_here, SUFFIX, SUFFIX)
    )
    inner = jnp.einsum("rhts,rshp->rthp", weight, chan, preferred_element_type=jnp.float32)
    grouped_state = start_state.reshape(
        requests_here, state_size, groups_here, per_group * head_width
    )
    carried = jnp.einsum(
        "rtgn,rngq->rtgq", c_part, grouped_state, preferred_element_type=jnp.float32
    )
    carried = (
        carried.reshape(requests_here, SUFFIX, heads_here, head_width) * jnp.exp(cum)[:, :, :, None]
    )
    chan_f = chan.astype(jnp.float32)
    mixed = (inner + carried + skip_gain[None, None, :, None] * chan_f) * live[:, :, None, None]
    mixed = mixed.astype(jnp.bfloat16).reshape(token_count, heads_here * head_width)
    factor = jnp.exp(cum[:, -1:, :] - cum) * step
    scaled = (chan_f * factor[:, :, :, None]).astype(jnp.bfloat16)
    scaled = scaled.reshape(requests_here, SUFFIX, groups_here, per_group * head_width)
    gained = jnp.einsum("rsgn,rsgq->rngq", b_part, scaled, preferred_element_type=jnp.float32)
    gained = gained.reshape(requests_here, state_size, heads_here * head_width)
    keep = jnp.repeat(jnp.exp(cum[:, -1, :]), head_width, axis=1)
    final_state = gained + keep[:, None, :] * start_state.astype(jnp.float32)
    return (mixed, final_state.astype(jnp.bfloat16))


def solution(mesh):
    return jax.shard_map(
        body,
        mesh=mesh,
        in_specs=(
            P("cache", None),
            P("cache", "head"),
            P("cache", "head", None),
            P("cache", "head"),
            P("head"),
            P("head"),
            P("head"),
            P("cache", "head", None),
            P(),
            P(),
            P("cache"),
        ),
        out_specs=(P("cache", "head"), P("cache", None, "head")),
        check_vma=False,
    )
```

profile of v0, /device:TPU:0, one launch (start us, length us, event | category | flops | bytes accessed | tf_op | source)
XLA Modules:
  0.0 583.7 jit_solution(9297158364628190671)
XLA Ops:
  10.3 8.0 %gather_fusion = bf16[8,64,8192]{2,1,0:T(8,128)(2,1)} fusion(bf16[8,64,8192]{2,1,0:T(8,128)(2,1)} %param.18, s32[1024]{0:T(1024)S(1)} %pad_clamp_fusion.1), kind=kCustom, calls=%fused_computation | custom fusion | bytes 16777248 | tf_op jit(solution)/shard_map/jit(_take)/gather | solution.py:35
  18.4 14.9 %gather.13 = bf16[8,64,4,2048]{3,2,1,0:T(4,128)(2,1)} reshape(bf16[8,64,8192]{2,1,0:T(8,128)(2,1)} %gather_fusion) | data formatting | bytes 16777216 | tf_op jit(solution)/shard_map/jit(_take)/gather | solution.py:35
  39.5 144.1 %all_to_all.20 = bf16[8,64,4,2048]{3,2,1,0:T(4,128)(2,1)} all-to-all(bf16[8,64,4,2048]{3,2,1,0:T(4,128)(2,1)S(1)} %select_select_fusion), channel_id=1, replica_groups=mesh['cache'=8,'head'=4] {'cache'}, dimensions={0} | all-to-all | bytes 16777216 | tf_op jit(solution)/shard_map/all_to_all | solution.py:42
  183.6 12.2 %copy.85 = bf16[8,64,4,2048]{3,1,0,2:T(8,128)(2,1)} copy(bf16[8,64,4,2048]{3,2,1,0:T(4,128)(2,1)} %all_to_all.20) | data formatting | bytes 16777216 | tf_op jit(solution)/shard_map/all_to_all | solution.py:42
  201.9 11.7 %all_gather.11 = bf16[8192,32]{0,1:T(8,128)(2,1)S(1)} all-gather(bf16[1024,32]{0,1:T(8,128)(2,1)S(1)} %copy-done.6), channel_id=1, replica_groups=mesh['cache'=8,'head'=4] {'cache'}, dimensions={0}, use_global_device_ids=true | all-gather | bytes 589824 | tf_op jit(solution)/shard_map/all_gather | solution.py:20
  213.7 8.4 %convolution_bitcast_fusion = f32[4,6,8,128]{3,2,1,0:T(8,128)S(1)} fusion(bf16[768,8192]{1,0:T(8,128)(2,1)} %param.11, bf16[8192,32]{0,1:T(8,128)(2,1)S(1)} %all_gather.11), kind=kOutput, calls=%fused_computation.23 | convolution fusion | flops 402653184 | bytes 13205504 | tf_op jit(solution)/shard_map/dot_general | solution.py:25
  225.0 158.8 %all-to-all-done.1 = bf16[8,64,4,2048]{3,1,0,2:T(8,128)(2,1)} async-done(((bf16[8,64,4,2048]{3,1,0,2:T(8,128)(2,1)}), bf16[8,64,4,2048]{3,1,0,2:T(8,128)(2,1)}, u32[]{:S(2)}, u32[]{:S(2)}) %all-to-all-start.1) | async-done | bytes 8388640 | tf_op jit(solution)/shard_map/all_to_all | solution.py:41
  383.8 8.3 %copy.86 = bf16[8,64,4,2048]{3,1,2,0:T(8,128)(2,1)} copy(bf16[8,64,4,2048]{3,1,0,2:T(8,128)(2,1)} %all-to-all-done.1) | data formatting | bytes 16777216 | tf_op jit(solution)/shard_map/all_to_all | solution.py:41
  392.1 7.6 %gather_fusion.1 = bf16[6,256,2048]{2,1,0:T(8,128)(2,1)} fusion(bf16[8,256,2048]{2,1,0:T(8,128)(2,1)} %bitcast.67, s32[1024]{0:T(1024)S(1)} %pad_clamp_fusion), kind=kCustom, calls=%fused_computation.1 | custom fusion | bytes 12582936 | tf_op jit(solution)/shard_map/jit(_take)/gather | solution.py:49
  399.7 8.6 %copy.95 = bf16[6,256,2048]{1,2,0:T(8,128)(2,1)} copy(bf16[6,256,2048]{2,1,0:T(8,128)(2,1)} %gather_fusion.1) | data formatting | bytes 12582912 | tf_op jit(solution)/shard_map/jit(_take)/gather | solution.py:49
  408.3 11.4 %copy.104 = bf16[1024,8,2,512]{3,1,2,0:T(8,128)(2,1)S(1)} copy(bf16[1024,8,2,512]{3,2,1,0:T(2,128)(2,1)} %bitcast.69) | data formatting | bytes 33554432
  419.7 16.2 %convolution_convert_fusion.1 = bf16[768,1024]{1,0:T(8,128)(2,1)S(1)} fusion(bf16[768,8192]{1,0:T(8,128)(2,1)} %param.11, bf16[8192,1024]{1,0:T(8,128)(2,1)S(1)} %bitcast.70), kind=kOutput, calls=%fused_computation.22 | convolution fusion | flops 12885688320 | bytes 30932992 | tf_op jit(solution)/shard_map/dot_general | solution.py:24
  440.4 7.2 %fusion.5 = f32[6,2,1024,128]{3,2,1,0:T(8,128)} fusion(bf16[6,256,2,1024]{1,3,2,0:T(8,128)(2,1)} %bitcast.73, pred[6]{0:T(512)(128)(4,1)S(1)} %get-tuple-element.10, bf16[6,128,2,256]{3,2,1,0:T(2,128)(2,1)S(1)} %get-tuple-element.13), kind=kOutput, calls=%fused_computation.12 | convolution fusion | flops 808452096 | bytes 13369350 | tf_op jit(solution)/shard_map/rtgn,rngq->rtgq/dot_general | solution.py:79
  447.7 31.7 %convolution_convert_fusion = bf16[768,2048]{1,0:T(8,128)(2,1)S(1)} fusion(bf16[768,8192]{1,0:T(8,128)(2,1)} %param.11, bf16[8192,2048]{1,0:T(8,128)(2,1)} %all-gather.3.cloned.1.call-done), kind=kOutput, calls=%fused_computation.20 | convolution fusion | flops 25771376640 | bytes 49283072 | tf_op jit(solution)/shard_map/dot_general | solution.py:23
  479.3 7.2 %reshape.172 = f32[6,128,2,1024]{3,2,1,0:T(2,128)} reshape(bf16[768,2048]{1,0:T(8,128)(2,1)S(1)} %convolution_convert_fusion) | data formatting | bytes 9437184 | tf_op jit(solution)/shard_map/convert_element_type | solution.py:85
  486.6 7.5 %reshape.190 = bf16[6,128,32,64]{3,2,1,0:T(8,128)(2,1)} reshape(bf16[768,2048]{1,0:T(8,128)(2,1)S(1)} %convolution_convert_fusion) | data formatting | bytes 6291456 | tf_op jit(solution)/shard_map/reshape | solution.py:50
  494.1 10.2 %copy.92 = f32[6,128,2,1024]{1,3,2,0:T(8,128)} copy(f32[6,128,2,1024]{3,2,1,0:T(2,128)} %reshape.172) | data formatting | bytes 12582912 | tf_op jit(solution)/shard_map/convert_element_type | solution.py:85
  504.3 9.0 %copy.84 = bf16[6,128,32,64]{1,3,2,0:T(8,128)(2,1)} copy(bf16[6,128,32,64]{3,2,1,0:T(8,128)(2,1)} %reshape.190) | data formatting | bytes 6291456 | tf_op jit(solution)/shard_map/reshape | solution.py:50
  517.2 6.3 %fusion.14 = f32[6,2,1024,256]{3,2,1,0:T(8,128)} fusion(bf16[6,128,2,1024]{1,3,2,0:T(8,128)(2,1)S(1)} %fusion.1, bf16[6,128,2,256]{3,2,1,0:T(2,128)(2,1)S(1)} %copy-done.2), kind=kOutput, calls=%fused_computation.24 | convolution fusion | flops 805306368 | bytes 16515072 | tf_op jit(solution)/shard_map/rsgn,rsgq->rngq/dot_general | solution.py:91
  523.5 12.9 %copy.93 = f32[6,256,2048]{2,1,0:T(8,128)} copy(f32[6,256,2048]{1,2,0:T(8,128)} %bitcast.66) | data formatting | bytes 25165824 | tf_op jit(solution)/shard_map/reshape | solution.py:92
  538.2 9.0 %fusion.4 = bf16[6,128,32,64]{1,3,2,0:T(8,128)(2,1)S(1)} fusion(bf16[6,128,32,64]{1,3,2,0:T(8,128)(2,1)S(1)} %copy-done.4, f32[6,128,32,64]{1,3,2,0:T(8,128)} %bitcast.76, f32[6,128]{1,0:T(8,128)S(1)} %fusion.21, f32[32]{0:T(128)S(1)} %copy-done.13, f32[6,128,32]{1,2,0:T(8,128)S(1)} %copy.88, f32[6,32,128,128]{3,2,1,0:T(8,128)S(1)} %bitcast.71, ...), kind=kOutput, calls=%fused_computation.11 | convolution fusion | flops 432537600 | bytes 25480320 | tf_op jit(solution)/shard_map/rhts,rshp->rthp/dot_general | solution.py:75
  547.3 9.1 %copy.96 = bf16[6,128,32,64]{3,2,1,0:T(8,128)(2,1)} copy(bf16[6,128,32,64]{1,3,2,0:T(8,128)(2,1)S(1)} %fusion.4) | data formatting | bytes 6291456
  556.4 9.8 %reshape.189 = bf16[768,2048]{1,0:T(8,128)(2,1)} reshape(bf16[6,128,32,64]{3,2,1,0:T(8,128)(2,1)} %copy.96) | data formatting | bytes 6291456
  566.2 10.4 %add_convert_fusion = bf16[6,256,2048]{2,1,0:T(8,128)(2,1)} fusion(f32[6,256,2048]{2,1,0:T(8,128)} %copy.93, bf16[6,256,2048]{2,1,0:T(8,128)(2,1)} %gather_fusion.1, f32[6,2048]{1,0:T(8,128)S(1)} %copy-done.5, pred[6]{0:T(512)(128)(4,1)S(1)} %get-tuple-element.10), kind=kLoop, calls=%fused_computation.2 | loop fusion | flops 15728640 | bytes 25214982 | tf_op jit(solution)/shard_map/convert_element_type | solution.py:95
  (70 shorter events, 28.6 us)
Async XLA Ops:
  7.2 1.5 copy-start.10
  7.2 2.1 copy-start.11
  7.2 401.1 %all-gather.5.cloned.1.call-start = ((), (), s32[]{:S(2)}) async-start(), calls=%async_computation.3 | async-start | bytes 18874368 | tf_op jit(solution)/shard_map/all_gather | solution.py:19
  7.9 439.7 %all-gather.3.cloned.1.call-start = ((), (), s32[]{:S(2)}) async-start(), calls=%async_computation.2 | async-start | bytes 37748736 | tf_op jit(solution)/shard_map/all_gather | solution.py:18
  195.8 6.1 %copy-start.6 = (bf16[1024,32]{0,1:T(8,128)(2,1)S(1)}, bf16[1024,32]{0,1:T(8,128)(2,1)}, u32[]{:S(2)}) copy-start(bf16[1024,32]{0,1:T(8,128)(2,1)} %param.14) | copy-start | bytes 196612
  195.8 17.8 %copy-start.12 = (f32[32]{0:T(128)S(1)}, f32[32]{0:T(128)}, u32[]{:S(2)}) copy-start(f32[32]{0:T(128)} %param.16) | copy-start | bytes 388
  195.8 17.8 %copy-start.9 = (s32[6]{0:T(128)S(1)}, s32[6]{0:T(128)}, u32[]{:S(2)}) copy-start(s32[6]{0:T(128)} %param.21) | copy-start | bytes 76
  195.8 188.0 %all-to-all-start.1 = ((bf16[8,64,4,2048]{3,1,0,2:T(8,128)(2,1)}), bf16[8,64,4,2048]{3,1,0,2:T(8,128)(2,1)}, u32[]{:S(2)}, u32[]{:S(2)}) async-start(bf16[8,64,4,2048]{3,1,0,2:T(8,128)(2,1)} %copy.85), calls=%async_computation.1 | async-start | bytes 16777216 | tf_op jit(solution)/shard_map/all_to_all | solution.py:41
  213.7 8.4 %copy-start.8 = (f32[32]{0:T(128)S(1)}, f32[32]{0:T(128)}, u32[]{:S(2)}) copy-start(f32[32]{0:T(128)} %param.15) | copy-start | bytes 388
  438.2 0.9 copy-start.1
  513.3 2.8 copy-start
  516.1 1.1 copy-start.2
  523.5 12.9 %copy-start.3 = (f32[6,2,128,128]{3,2,1,0:T(8,128)S(1)}, f32[6,2,128,128]{3,2,1,0:T(8,128)}, u32[]{:S(2)}) copy-start(f32[6,2,128,128]{3,2,1,0:T(8,128)} %fusion.16) | copy-start | bytes 2359300
  536.3 1.9 copy-start.4
  536.3 1.9 copy-start.7
  536.4 1.9 copy-start.13
  556.4 9.8 %copy-start.5 = (f32[6,2048]{1,0:T(8,128)S(1)}, f32[6,2048]{1,0:T(8,128)}, u32[]{:S(2)}) copy-start(f32[6,2048]{1,0:T(8,128)} %mul.116) | copy-start | bytes 147460
Sparse Core Ops, SparseCore 0:
  9.9 174.0 all-gather.4
  185.9 164.2 all-gather.2
where the time goes:
time: 591 us; the launch traced here: 584 us
  waiting for transfers between devices  160 us (27%)
  blocking collectives  156 us (26%)
  local copies, waits for them, and re-layouts  147 us (25%)
  matrix products  80.1 us (14%)
  other arithmetic  19.6 us (3%)
  between operations  14.5 us (2%)
  starting transfers between devices  6.19 us (1%)
    all_to_all x1, waiting for transfers between devices, body(): lax.all_to_all(lax.all_to_all(blocks, 'cache', split_axis=0, concat_axis=...  159 us
    all_to_all x1, blocking collectives, body(): lax.all_to_all(blocks, 'cache', split_axis=0, concat_axis=0, tiled=True)  144 us
    unnamed x33, local copies, waits for them, and re-layouts  34.9 us
    dot_general x1, matrix products, body(): part_x = jnp.dot(tokens, pieces[0], preferred_element_type=jnp.float32)  31.7 us
    gather x2, local copies, waits for them, and re-layouts, body(): tiles = jnp.take(pool, chosen_slot, axis=0)  22.9 us
    convert_element_type x2, local copies, waits for them, and re-layouts, body(): chan_f = chan.astype(jnp.float32)  17.4 us
    reshape x2, local copies, waits for them, and re-layouts, body(): part_x.astype(jnp.bfloat16)  16.5 us
    dot_general x1, matrix products, body(): jnp.dot(tokens, pieces[1].reshape(row_count, -1), preferred_element_type=...  16.2 us
  transfers between devices with their start and end apart: 3, of which 1 were waited for; matrix products, arithmetic and copies ran while one was open for 20% of the time, Pallas kernels for 0%

commit v1 on v0

v1 whole, which is shorter than its diff:
```python
import functools

import jax
import jax.numpy as jnp
from jax import lax
from jax.experimental import pallas as pl
from jax.experimental.pallas import tpu as pltpu
from jax.sharding import PartitionSpec as P

SUFFIX = 128
LANES = 128


def pick_kernel(index_ref, src_ref, out_ref):
    del index_ref
    width = out_ref.shape[-1]
    for part in range(out_ref.shape[1]):
        out_ref[0, part] = src_ref[0, :, part * width : (part + 1) * width]


def pick_for_owners(pool, chosen, parts):
    count = chosen.shape[0]
    _, rows, cols = pool.shape
    width = cols // parts
    return pl.pallas_call(
        pick_kernel,
        out_shape=jax.ShapeDtypeStruct((count, parts, rows, width), pool.dtype),
        grid_spec=pltpu.PrefetchScalarGridSpec(
            num_scalar_prefetch=1,
            grid=(count,),
            in_specs=[pl.BlockSpec((1, rows, cols), lambda i, s: (s[i], 0, 0))],
            out_specs=pl.BlockSpec((1, parts, rows, width), lambda i, s: (i, 0, 0, 0)),
        ),
        cost_estimate=pl.CostEstimate(
            flops=0, bytes_accessed=4 * count * rows * cols, transcendentals=0
        ),
    )(chosen, pool)


def turn_kernel(index_ref, src_ref, out_ref):
    del index_ref
    out_ref[:, 0] = src_ref[0]


def pick_for_requests(received, my_owners):
    count = my_owners.shape[0]
    _, parts, rows, width = received.shape
    return pl.pallas_call(
        turn_kernel,
        out_shape=jax.ShapeDtypeStruct((parts, count, rows, width), received.dtype),
        grid_spec=pltpu.PrefetchScalarGridSpec(
            num_scalar_prefetch=1,
            grid=(count,),
            in_specs=[pl.BlockSpec((1, parts, rows, width), lambda i, s: (s[i], 0, 0, 0))],
            out_specs=pl.BlockSpec((parts, 1, rows, width), lambda i, s: (0, i, 0, 0)),
        ),
        cost_estimate=pl.CostEstimate(
            flops=0, bytes_accessed=4 * count * parts * rows * width, transcendentals=0
        ),
    )(my_owners, received)


def ssd_kernel(first, heads, width, n_carry, *refs):
    (chan_ref, bc_ref, cum_ref, cum_t_ref, step_t_ref, factor_ref, grown_ref, live_ref,
     keep_ref, gain_ref, state_ref) = refs[:11]
    mixed_ref, final_ref, scaled_ref = refs[11 + n_carry :]
    state_size = bc_ref.shape[1] // 2
    b_part = bc_ref[:, :state_size]
    c_part = bc_ref[:, state_size:]
    scores = lax.dot_general(
        c_part, b_part, (((1,), (1,)), ((), ())), preferred_element_type=jnp.float32
    )
    state = state_ref[...].reshape(state_size, heads * width)
    carried = jnp.dot(c_part, state, preferred_element_type=jnp.float32)
    here = lax.broadcasted_iota(jnp.int32, (SUFFIX, SUFFIX), 0)
    there = lax.broadcasted_iota(jnp.int32, (SUFFIX, SUFFIX), 1)
    causal = here >= there
    per_tile = LANES // width
    lane_head = lax.broadcasted_iota(jnp.int32, (SUFFIX, LANES), 1) // width
    live = live_ref[...]

    def spread_heads(ref, head):
        value = jnp.broadcast_to(ref[:, head : head + 1], (SUFFIX, LANES))
        for k in range(1, per_tile):
            value = jnp.where(lane_head == k, ref[:, head + k : head + k + 1], value)
        return value

    for tile in range(heads // per_tile):
        head = first + tile * per_tile
        lanes = slice(tile * LANES, (tile + 1) * LANES)
        chan = chan_ref[:, lanes].astype(jnp.float32)
        weights, values = [], []
        for k in range(per_tile):
            h = head + k
            spread = cum_ref[:, h : h + 1] - cum_t_ref[0, h : h + 1, :]
            decay = jnp.exp(jnp.where(causal, spread, -1e30))
            weights.append((scores * decay * step_t_ref[0, h : h + 1, :]).astype(jnp.bfloat16))
            values.append(jnp.where(lane_head == k, chan, 0.0).astype(jnp.bfloat16))
        inner = jnp.dot(
            jnp.concatenate(weights, axis=1),
            jnp.concatenate(values, axis=0),
            preferred_element_type=jnp.float32,
        )
        mixed = inner + carried[:, lanes] * spread_heads(grown_ref, head)
        mixed = (mixed + gain_ref[:, lanes] * chan) * live
        mixed_ref[:, lanes] = mixed.astype(jnp.bfloat16)
        scaled_ref[:, lanes] = (chan * spread_heads(factor_ref, head)).astype(jnp.bfloat16)
    gained = lax.dot_general(
        b_part, scaled_ref[...], (((0,), (0,)), ((), ())), preferred_element_type=jnp.float32
    )
    final_ref[0] = (gained + keep_ref[0] * state.astype(jnp.float32)).astype(jnp.bfloat16)


def ssd(first, heads, group, chan, proj_bc, small, state, carry, total_cols):
    cum, cum_t, step_t, factor, grown, live, keep, gain = small
    tokens, cols = chan.shape
    requests = tokens // SUFFIX
    all_heads = cum.shape[1]
    parts, _, rows, _ = state.shape
    state_size = parts * rows
    width = cols // heads
    block = first * width // cols
    in_specs = [
        pl.BlockSpec((SUFFIX, cols), lambda r: (r, 0)),
        pl.BlockSpec((SUFFIX, 2 * state_size), lambda r: (r, group)),
        pl.BlockSpec((SUFFIX, all_heads), lambda r: (r, 0)),
        pl.BlockSpec((1, all_heads, SUFFIX), lambda r: (r, 0, 0)),
        pl.BlockSpec((1, all_heads, SUFFIX), lambda r: (r, 0, 0)),
        pl.BlockSpec((SUFFIX, all_heads), lambda r: (r, 0)),
        pl.BlockSpec((SUFFIX, all_heads), lambda r: (r, 0)),
        pl.BlockSpec((SUFFIX, 1), lambda r: (r, 0)),
        pl.BlockSpec((1, 1, cols), lambda r: (r, 0, block)),
        pl.BlockSpec((1, cols), lambda r: (0, block)),
        pl.BlockSpec((parts, 1, rows, cols), lambda r: (0, r, 0, block)),
    ]
    aliases = {}
    if carry:
        in_specs += [pl.BlockSpec(memory_space=pl.ANY)] * len(carry)
        aliases = {11 + i: i for i in range(len(carry))}
    flops = 2 * tokens * cols * (2 * state_size + 2 * SUFFIX)
    return pl.pallas_call(
        functools.partial(ssd_kernel, first, heads, width, len(carry)),
        out_shape=(
            jax.ShapeDtypeStruct((tokens, total_cols), jnp.bfloat16),
            jax.ShapeDtypeStruct((requests, state_size, total_cols), jnp.bfloat16),
        ),
        grid=(requests,),
        in_specs=in_specs,
        out_specs=(
            pl.BlockSpec((SUFFIX, cols), lambda r: (r, block)),
            pl.BlockSpec((1, state_size, cols), lambda r: (r, 0, block)),
        ),
        scratch_shapes=[pltpu.VMEM((SUFFIX, cols), jnp.bfloat16)],
        input_output_aliases=aliases,
        compiler_params=pltpu.CompilerParams(vmem_limit_bytes=48 * 1024 * 1024),
        cost_estimate=pl.CostEstimate(
            flops=flops,
            bytes_accessed=4 * cols * (tokens + requests * state_size),
            transcendentals=tokens * SUFFIX * heads,
        ),
    )(chan, proj_bc, cum, cum_t, step_t, factor, grown, live, keep, gain, state, *carry)


def body(tokens, w_x, w_bc, w_dt, dt_bias, decay_log, skip_gain, pool, owners, slots, offsets):
    token_count = tokens.shape[0]
    requests_here = token_count // SUFFIX
    heads_here = dt_bias.shape[0]
    groups_here = w_bc.shape[1]
    per_group = heads_here // groups_here
    total_cols = w_x.shape[1]
    head_width = total_cols // heads_here
    bc_cols = w_bc.shape[1] * w_bc.shape[2]
    cache_count = lax.axis_size("cache")
    head_count = lax.axis_size("head")
    my_cache = lax.axis_index("cache")

    chunks = []
    for group in range(groups_here):
        pieces = 2 if group == groups_here - 1 else 1
        size = per_group // pieces
        chunks += [(group * per_group + i * size, size, group) for i in range(pieces)]

    local_small = jnp.concatenate([w_bc.reshape(w_bc.shape[0], bc_cols), w_dt], axis=1)
    w_small = lax.all_gather(local_small, "cache", axis=0, tiled=True)
    w_parts = [
        lax.all_gather(
            w_x[:, first * head_width : (first + size) * head_width], "cache", axis=0, tiled=True
        )
        for first, size, _ in chunks
    ]

    owner_table = owners[:, 0].reshape(cache_count, requests_here)
    slot_table = slots[:, 0].reshape(cache_count, requests_here)
    chosen_slot = jnp.sum(jnp.where(owner_table == my_cache, slot_table, 0), axis=1)
    my_owners = lax.dynamic_slice_in_dim(owners[:, 0], my_cache * requests_here, requests_here)
    blocks = pick_for_owners(pool, chosen_slot, head_count)
    received = lax.all_to_all(blocks, "cache", split_axis=0, concat_axis=0, tiled=True)
    wanted = pick_for_requests(received, my_owners)
    state = lax.all_to_all(wanted, "head", split_axis=0, concat_axis=0, tiled=True)

    part_small = jnp.dot(tokens, w_small, preferred_element_type=jnp.float32)
    proj_bc = part_small[:, :bc_cols].astype(jnp.bfloat16)
    dt_raw = part_small[:, bc_cols:].reshape(requests_here, SUFFIX, heads_here)
    positions = jnp.arange(SUFFIX, dtype=jnp.int32)
    live = (positions[None, :] >= offsets[:, None]).astype(jnp.float32)
    step = jax.nn.softplus(dt_raw + dt_bias[None, None, :]) * live[:, :, None]
    rate = -jnp.exp(decay_log)[None, None, :] * step
    cum = jnp.cumsum(rate, axis=1)
    last = cum[:, -1:, :]
    factor = jnp.exp(last - cum) * step
    small = (
        cum.reshape(token_count, heads_here),
        jnp.transpose(cum, (0, 2, 1)),
        jnp.transpose(step, (0, 2, 1)),
        factor.reshape(token_count, heads_here),
        jnp.exp(cum).reshape(token_count, heads_here),
        live.reshape(token_count, 1),
        jnp.repeat(jnp.exp(last), head_width, axis=2),
        jnp.repeat(skip_gain, head_width)[None, :],
    )

    carry = ()
    for (first, size, group), w_part in zip(chunks, w_parts):
        chan = jnp.dot(tokens, w_part, preferred_element_type=jnp.float32).astype(jnp.bfloat16)
        carry = ssd(first, size, group, chan, proj_bc, small, state, carry, total_cols)
    return tuple(carry)


def solution(mesh):
    return jax.shard_map(
        body,
        mesh=mesh,
        in_specs=(
            P("cache", None),
            P("cache", "head"),
            P("cache", "head", None),
            P("cache", "head"),
            P("head"),
            P("head"),
            P("head"),
            P("cache", "head", None),
            P(),
            P(),
            P("cache"),
        ),
        out_specs=(P("cache", "head"), P("cache", None, "head")),
        check_vma=False,
    )
```

time: 591 us -> 437 us (0.74); the launches traced: 584 us -> 436 us
  blocking collectives: 156 us -> 0 us
  local copies, waits for them, and re-layouts: 147 us -> 12 us
  waiting for transfers between devices: 160 us -> 284 us
  Pallas kernels: 0 us -> 41.5 us
  other arithmetic: 19.6 us -> 4.25 us
  matrix products: 80.1 us -> 67.5 us
    all_gather x2 -> x4, waiting for transfers between devices: 0.01 us -> 154 us  [the longest x1 81.1 us: body(): w_small = lax.all_gather(local_small, 'cache', axis=0, tiled=True)]
    all_to_all x1 -> x0, blocking collectives: 144 us -> none  [body(): lax.all_to_all(blocks, 'cache', split_axis=0, concat_axis=0, tiled=True)]
    pallas_call x0 -> x5, Pallas kernels: none -> 41.5 us  [the longest x3 24.1 us: ssd(): pl.pallas_call(functools.partial(ssd_kernel, first, heads, width, len(car...]
    gather x4 -> x0, local copies, waits for them, and re-layouts: 39.1 us -> none  [the longest x2 22.9 us: body(): tiles = jnp.take(pool, chosen_slot, axis=0)]
    unnamed x33 -> x29, local copies, waits for them, and re-layouts: 34.9 us -> 4.07 us
    reshape x4 -> x1, local copies, waits for them, and re-layouts: 30.6 us -> 0.14 us  [body(): dt_raw = part_small[:, bc_cols:].reshape(requests_here, SUFFIX, heads_here)]
    all_to_all x1 -> x2, waiting for transfers between devices: 159 us -> 130 us  [the longest x1 130 us: body(): lax.all_to_all(blocks, 'cache', split_axis=0, concat_axis=0, tiled=True)]
    all_to_all x2 -> x0, local copies, waits for them, and re-layouts: 20.4 us -> none  [the longest x1 12.2 us: body(): lax.all_to_all(blocks, 'cache', split_axis=0, concat_axis=0, tiled=True)]
  transfers between devices with their start and end apart: 3 -> 6, of which waited for: 1 -> 3; matrix products, arithmetic and copies ran while one was open for 20% -> 18% of each run, Pallas kernels for 0% -> 4%
where the time goes in v1:
time: 437 us; the launch traced here: 436 us
  waiting for transfers between devices  284 us (65%)
  matrix products  67.5 us (15%)
  Pallas kernels  41.5 us (9%)
  between operations  14 us (3%)
  local copies, waits for them, and re-layouts  12 us (3%)
  starting transfers between devices  11.9 us (3%)
    all_to_all x1, waiting for transfers between devices, body(): lax.all_to_all(blocks, 'cache', split_axis=0, concat_axis=0, tiled=True)  130 us
    all_gather x1, waiting for transfers between devices, body(): w_small = lax.all_gather(local_small, 'cache', axis=0, tiled=True)  81.1 us
    all_gather x3, waiting for transfers between devices, body(): lax.all_gather(w_x[:, first * head_width:(first + size) * head_width], 'c...  72.7 us
    dot_general x3, matrix products, body(): jnp.dot(tokens, w_part, preferred_element_type=jnp.float32)  46.9 us
    pallas_call x3, Pallas kernels, ssd(): pl.pallas_call(functools.partial(ssd_kernel, first, heads, width, len(car...  24.1 us
    dot_general x1, matrix products, body(): part_small = jnp.dot(tokens, w_small, preferred_element_type=jnp.float32)  20.6 us
    pallas_call x1, Pallas kernels, pick_for_owners(): pl.pallas_call(pick_kernel, out_shape=jax.ShapeDtypeStruct((count, parts,...  9.86 us
  transfers between devices with their start and end apart: 6, of which 3 were waited for; matrix products, arithmetic and copies ran while one was open for 18% of the time, Pallas kernels for 4%

profile of v1, /device:TPU:0, one launch (start us, length us, event | category | flops | bytes accessed | tf_op | source)
XLA Modules:
  0.0 435.6 jit_solution(13455491318470929964)
XLA Ops:
  7.2 3.2 fusion.9
  10.5 0.7 all-gather.5.cloned.1.call-update
  11.2 3.1 slice.24
  14.6 0.6 copy.33
  15.1 1.6 pad_maximum_fusion
  16.9 0.6 reduce_sum.9.index_ref
  17.6 9.9 %shard_map.122 = bf16[8,4,64,2048]{3,2,1,0:T(8,128)(2,1)} custom-call(s32[8]{0:T(128)} %reduce_sum.9.index_ref, bf16[8,64,8192]{2,1,0:T(8,128)(2,1)} %src_ref.1), custom_call_target="tpu_custom_call" | custom-call | bytes 16777216 | tf_op jit(solution)/shard_map/pallas_call | solution.py:25
  27.4 5.5 %all-to-all-start = ((bf16[8,4,64,2048]{3,2,1,0:T(8,128)(2,1)}), bf16[8,4,64,2048]{3,2,1,0:T(8,128)(2,1)}, u32[]{:S(2)}, u32[]{:S(2)}) async-start(bf16[8,4,64,2048]{3,2,1,0:T(8,128)(2,1)} %shard_map.122), calls=%async_computation | async-start | bytes 16777216 | tf_op jit(solution)/shard_map/all_to_all | solution.py:197
  33.4 0.6 dynamic-slice_bitcast_fusion.index_ref
  34.0 129.9 %all-to-all-done.src_ref = bf16[8,4,64,2048]{3,2,1,0:T(8,128)(2,1)} async-done(((bf16[8,4,64,2048]{3,2,1,0:T(8,128)(2,1)}), bf16[8,4,64,2048]{3,2,1,0:T(8,128)(2,1)}, u32[]{:S(2)}, u32[]{:S(2)}) %all-to-all-start) | async-done | bytes 8388640 | tf_op jit(solution)/shard_map/all_to_all | solution.py:197
  163.9 7.6 %shard_map.123 = bf16[4,6,64,2048]{3,2,1,0:T(8,128)(2,1)} custom-call(s32[6]{0:T(128)} %dynamic-slice_bitcast_fusion.index_ref, bf16[8,4,64,2048]{3,2,1,0:T(8,128)(2,1)} %all-to-all-done.src_ref), custom_call_target="tpu_custom_call" | custom-call | bytes 12582912 | tf_op jit(solution)/shard_map/pallas_call | solution.py:48
  171.5 6.2 %all-to-all-start.1 = ((bf16[4,6,64,2048]{3,2,1,0:T(8,128)(2,1)}), bf16[4,6,64,2048]{3,2,1,0:T(8,128)(2,1)}, u32[]{:S(2)}, u32[]{:S(2)}) async-start(bf16[4,6,64,2048]{3,2,1,0:T(8,128)(2,1)} %shard_map.123), calls=%async_computation.1 | async-start | bytes 12582912 | tf_op jit(solution)/shard_map/all_to_all | solution.py:199
  177.7 13.0 %convolution_convert_fusion.1.refs_0_ = bf16[768,512]{1,0:T(8,128)(2,1)} fusion(bf16[768,8192]{1,0:T(8,128)(2,1)} %param.11, bf16[8192,512]{1,0:T(8,128)(2,1)} %all-gather.9.cloned.1.call-done), kind=kOutput, calls=%fused_computation.4 | convolution fusion | flops 6442844160 | bytes 21757952 | tf_op jit(solution)/shard_map/dot_general | solution.py:224
  190.7 14.0 %convolution_convert_fusion.2.refs_0_ = bf16[768,512]{1,0:T(8,128)(2,1)} fusion(bf16[768,8192]{1,0:T(8,128)(2,1)} %param.11, bf16[8192,512]{1,0:T(8,128)(2,1)} %all-gather.5.cloned.1.call-done), kind=kOutput, calls=%fused_computation.5 | convolution fusion | flops 6442844160 | bytes 21757952 | tf_op jit(solution)/shard_map/dot_general | solution.py:224
  204.6 72.7 %all-gather.11.cloned.1.call-done = bf16[8192,1024]{1,0:T(8,128)(2,1)} async-done(((bf16[1024,1024]{1,0:T(8,128)(2,1)}), bf16[8192,1024]{1,0:T(8,128)(2,1)}) %all-gather.11.cloned.1.call-update) | async-done | bytes 16777232 | tf_op jit(solution)/shard_map/all_gather | solution.py:186
  277.3 20.0 %convolution_convert_fusion.refs_0_ = bf16[768,1024]{1,0:T(8,128)(2,1)} fusion(bf16[768,8192]{1,0:T(8,128)(2,1)} %param.11, bf16[8192,1024]{1,0:T(8,128)(2,1)} %all-gather.11.cloned.1.call-done), kind=kOutput, calls=%fused_computation.3 | convolution fusion | flops 12885688320 | bytes 30932992 | tf_op jit(solution)/shard_map/dot_general | solution.py:224
  297.3 81.1 %all-gather.7.cloned.1.call-done = bf16[8192,1056]{1,0:T(8,128)(2,1)} async-done(((bf16[1024,1056]{1,0:T(8,128)(2,1)}), bf16[8192,1056]{1,0:T(8,128)(2,1)}) %all-gather.7.cloned.1.call-update) | async-done | bytes 17301520 | tf_op jit(solution)/shard_map/all_gather | solution.py:184
  378.4 20.6 %convolution_bitcast_fusion = f32[768,1056]{1,0:T(8,128)S(1)} fusion(bf16[768,8192]{1,0:T(8,128)(2,1)} %param.11, bf16[8192,1056]{1,0:T(8,128)(2,1)} %all-gather.7.cloned.1.call-done), kind=kOutput, calls=%fused_computation | convolution fusion | flops 13287555072 | bytes 33128448 | tf_op jit(solution)/shard_map/dot_general | solution.py:201
  399.0 1.7 copy-done.4
  402.2 1.4 bitcast_exponential_fusion
  403.6 1.4 copy-done
  405.0 9.8 %shard_map.124 = (bf16[768,2048]{1,0:T(8,128)(2,1)}, bf16[6,256,2048]{2,1,0:T(8,128)(2,1)}) custom-call(bf16[768,1024]{1,0:T(8,128)(2,1)S(1)} %copy-done, bf16[768,1024]{1,0:T(8,128)(2,1)S(1)} %slice.31.refs_1_, f32[768,32]{1,0:T(8,128)S(1)} %bitcast.40, f32[6,32,128]{2,1,0:T(8,128)S(1)} %bitcast.46, f32[6,32,128]{2,1,0:T(8,128)S(1)} %get-tuple-element.16.refs_4_, ...), custom_call_target="tpu_custom_call" | custom-call | flops 1207959552 | bytes 9437184 | tf_op jit(solution)/shard_map/pallas_call | solution.py:141
  414.8 7.2 %shard_map.125 = (bf16[768,2048]{1,0:T(8,128)(2,1)}, bf16[6,256,2048]{2,1,0:T(8,128)(2,1)}) custom-call(bf16[768,512]{1,0:T(8,128)(2,1)S(1)} %copy-done.2, bf16[768,1024]{1,0:T(8,128)(2,1)S(1)} %slice.31.refs_1_, f32[768,32]{1,0:T(8,128)S(1)} %bitcast.41, f32[6,32,128]{2,1,0:T(8,128)S(1)} %bitcast.47, ...), custom_call_target="tpu_custom_call", output_to_operand_aliasing={{0}: (11, {}), {1}: (12, {})} | custom-call | flops 603979776 | bytes 4718592 | tf_op jit(solution)/shard_map/pallas_call | solution.py:141
  422.0 7.1 %shard_map.126 = (bf16[768,2048]{1,0:T(8,128)(2,1)}, bf16[6,256,2048]{2,1,0:T(8,128)(2,1)}) custom-call(bf16[768,512]{1,0:T(8,128)(2,1)S(1)} %copy-done.1, bf16[768,1024]{1,0:T(8,128)(2,1)S(1)} %slice.31.refs_1_, f32[768,32]{1,0:T(8,128)S(1)} %bitcast.42, f32[6,32,128]{2,1,0:T(8,128)S(1)} %bitcast.48, ...), custom_call_target="tpu_custom_call", output_to_operand_aliasing={{0}: (11, {}), {1}: (12, {})} | custom-call | flops 603979776 | bytes 4718592 | tf_op jit(solution)/shard_map/pallas_call | solution.py:141
  (52 shorter events, 2.4 us)
Async XLA Ops:
  7.2 7.2 %copy-start.5 = (bf16[1024,32]{0,1:T(8,128)(2,1)S(1)}, bf16[1024,32]{0,1:T(8,128)(2,1)}, u32[]{:S(2)}) copy-start(bf16[1024,32]{0,1:T(8,128)(2,1)} %param.14) | copy-start | bytes 196612
  7.2 7.4 %copy-start.3 = (bf16[1024,2,512]{2,1,0:T(2,128)(2,1)S(1)}, bf16[1024,2,512]{2,1,0:T(2,128)(2,1)}, u32[]{:S(2)}) copy-start(bf16[1024,2,512]{2,1,0:T(2,128)(2,1)} %param.13) | copy-start | bytes 6291460
  7.2 170.5 %all-gather.9.cloned.1.call-start = ((), (), s32[]{:S(2)}) async-start(), calls=%async_computation.4 | async-start | bytes 9437184 | tf_op jit(solution)/shard_map/all_gather | solution.py:186
  10.4 180.2 %all-gather.5.cloned.1.call-start = ((), (), s32[]{:S(2)}) async-start(), calls=%async_computation.2 | async-start | bytes 9437184 | tf_op jit(solution)/shard_map/all_gather | solution.py:186
  11.2 5.6 %copy-start.9 = (s32[48,1]{0,1:T(1,128)S(1)}, s32[48,1]{0,1:T(1,128)}, u32[]{:S(2)}) copy-start(s32[48,1]{0,1:T(1,128)} %param.20) | copy-start | bytes 580
  11.2 5.6 %copy-start.10 = (s32[48,1]{0,1:T(1,128)S(1)}, s32[48,1]{0,1:T(1,128)}, u32[]{:S(2)}) copy-start(s32[48,1]{0,1:T(1,128)} %param.19) | copy-start | bytes 580
  11.2 266.1 %all-gather.11.cloned.1.call-start = ((), (), s32[]{:S(2)}) async-start(), calls=%async_computation.5 | async-start | bytes 18874368 | tf_op jit(solution)/shard_map/all_gather | solution.py:186
  14.3 364.0 %all-gather.7.cloned.1.call-start = ((), (), s32[]{:S(2)}) async-start(), calls=%async_computation.3 | async-start | bytes 21233664 | tf_op jit(solution)/shard_map/all_gather | solution.py:184
  27.4 5.5 %copy-start.7 = (s32[6]{0:T(128)S(1)}, s32[6]{0:T(128)}, u32[]{:S(2)}) copy-start(s32[6]{0:T(128)} %param.21) | copy-start | bytes 76
  27.4 5.6 %copy-start.8 = (f32[32]{0:T(128)S(1)}, f32[32]{0:T(128)}, u32[]{:S(2)}) copy-start(f32[32]{0:T(128)} %param.17) | copy-start | bytes 388
  27.4 6.5 %copy-start.11 = (f32[32]{0:T(128)S(1)}, f32[32]{0:T(128)}, u32[]{:S(2)}) copy-start(f32[32]{0:T(128)} %param.16) | copy-start | bytes 388
  27.4 136.5 %all-to-all-start = ((bf16[8,4,64,2048]{3,2,1,0:T(8,128)(2,1)}), bf16[8,4,64,2048]{3,2,1,0:T(8,128)(2,1)}, u32[]{:S(2)}, u32[]{:S(2)}) async-start(bf16[8,4,64,2048]{3,2,1,0:T(8,128)(2,1)} %shard_map.122), calls=%async_computation | async-start | bytes 16777216 | tf_op jit(solution)/shard_map/all_to_all | solution.py:197
  171.5 232.1 %all-to-all-start.1 = ((bf16[4,6,64,2048]{3,2,1,0:T(8,128)(2,1)}), bf16[4,6,64,2048]{3,2,1,0:T(8,128)(2,1)}, u32[]{:S(2)}, u32[]{:S(2)}) async-start(bf16[4,6,64,2048]{3,2,1,0:T(8,128)(2,1)} %shard_map.123), calls=%async_computation.1 | async-start | bytes 12582912 | tf_op jit(solution)/shard_map/all_to_all | solution.py:199
  297.3 103.8 %copy-start.6 = (f32[32]{0:T(128)S(1)}, f32[32]{0:T(128)}, u32[]{:S(2)}) copy-start(f32[32]{0:T(128)} %param.15) | copy-start | bytes 388
  399.0 1.7 copy-start.4
  403.6 1.4 copy-start
  405.0 9.8 %copy-start.2 = (bf16[768,512]{1,0:T(8,128)(2,1)S(1)}, bf16[768,512]{1,0:T(8,128)(2,1)}, u32[]{:S(2)}) copy-start(bf16[768,512]{1,0:T(8,128)(2,1)} %convolution_convert_fusion.1.refs_0_) | copy-start | bytes 2359300
  414.8 7.2 %copy-start.1 = (bf16[768,512]{1,0:T(8,128)(2,1)S(1)}, bf16[768,512]{1,0:T(8,128)(2,1)}, u32[]{:S(2)}) copy-start(bf16[768,512]{1,0:T(8,128)(2,1)} %convolution_convert_fusion.2.refs_0_) | copy-start | bytes 2359300
Sparse Core Ops, SparseCore 0:
  10.5 102.1 all-gather.8
  114.6 70.6 all-gather.4
  187.2 90.0 all-gather.10
  279.6 98.7 all-gather.6

commit v2 on v1

--- a/solution.py
+++ b/solution.py
@@ -60,7 +60,8 @@
     )(my_owners, received)
 
 
-def ssd_kernel(first, heads, width, n_carry, *refs):
+def ssd_kernel(first, heads, width, n_carry, index_ref, *refs):
+    del index_ref
     (chan_ref, bc_ref, cum_ref, cum_t_ref, step_t_ref, factor_ref, grown_ref, live_ref,
      keep_ref, gain_ref, state_ref) = refs[:11]
     mixed_ref, final_ref, scaled_ref = refs[11 + n_carry :]
@@ -111,32 +112,34 @@
     final_ref[0] = (gained + keep_ref[0] * state.astype(jnp.float32)).astype(jnp.bfloat16)
 
 
-def ssd(first, heads, group, chan, proj_bc, small, state, carry, total_cols):
+def ssd(first, heads, group, chan, proj_bc, small, state, places, carry, total_cols):
     cum, cum_t, step_t, factor, grown, live, keep, gain = small
-    tokens, cols = chan.shape
+    tokens = chan.shape[0]
     requests = tokens // SUFFIX
     all_heads = cum.shape[1]
     parts, _, rows, _ = state.shape
     state_size = parts * rows
-    width = cols // heads
+    width = total_cols // all_heads
+    cols = heads * width
     block = first * width // cols
+    chan_block = block if chan.shape[1] == total_cols else 0
     in_specs = [
-        pl.BlockSpec((SUFFIX, cols), lambda r: (r, 0)),
-        pl.BlockSpec((SUFFIX, 2 * state_size), lambda r: (r, group)),
-        pl.BlockSpec((SUFFIX, all_heads), lambda r: (r, 0)),
-        pl.BlockSpec((1, all_heads, SUFFIX), lambda r: (r, 0, 0)),
-        pl.BlockSpec((1, all_heads, SUFFIX), lambda r: (r, 0, 0)),
-        pl.BlockSpec((SUFFIX, all_heads), lambda r: (r, 0)),
-        pl.BlockSpec((SUFFIX, all_heads), lambda r: (r, 0)),
-        pl.BlockSpec((SUFFIX, 1), lambda r: (r, 0)),
-        pl.BlockSpec((1, 1, cols), lambda r: (r, 0, block)),
-        pl.BlockSpec((1, cols), lambda r: (0, block)),
-        pl.BlockSpec((parts, 1, rows, cols), lambda r: (0, r, 0, block)),
+        pl.BlockSpec((SUFFIX, cols), lambda r, s: (r, chan_block)),
+        pl.BlockSpec((SUFFIX, 2 * state_size), lambda r, s: (r, group)),
+        pl.BlockSpec((SUFFIX, all_heads), lambda r, s: (r, 0)),
+        pl.BlockSpec((1, all_heads, SUFFIX), lambda r, s: (r, 0, 0)),
+        pl.BlockSpec((1, all_heads, SUFFIX), lambda r, s: (r, 0, 0)),
+        pl.BlockSpec((SUFFIX, all_heads), lambda r, s: (r, 0)),
+        pl.BlockSpec((SUFFIX, all_heads), lambda r, s: (r, 0)),
+        pl.BlockSpec((SUFFIX, 1), lambda r, s: (r, 0)),
+        pl.BlockSpec((1, 1, cols), lambda r, s: (r, 0, block)),
+        pl.BlockSpec((1, cols), lambda r, s: (0, block)),
+        pl.BlockSpec((parts, 1, rows, cols), lambda r, s: (0, s[r], 0, block)),
     ]
     aliases = {}
     if carry:
         in_specs += [pl.BlockSpec(memory_space=pl.ANY)] * len(carry)
-        aliases = {11 + i: i for i in range(len(carry))}
+        aliases = {12 + i: i for i in range(len(carry))}
     flops = 2 * tokens * cols * (2 * state_size + 2 * SUFFIX)
     return pl.pallas_call(
         functools.partial(ssd_kernel, first, heads, width, len(carry)),
@@ -144,13 +147,16 @@
             jax.ShapeDtypeStruct((tokens, total_cols), jnp.bfloat16),
             jax.ShapeDtypeStruct((requests, state_size, total_cols), jnp.bfloat16),
         ),
-        grid=(requests,),
-        in_specs=in_specs,
-        out_specs=(
-            pl.BlockSpec((SUFFIX, cols), lambda r: (r, block)),
-            pl.BlockSpec((1, state_size, cols), lambda r: (r, 0, block)),
-        ),
-        scratch_shapes=[pltpu.VMEM((SUFFIX, cols), jnp.bfloat16)],
+        grid_spec=pltpu.PrefetchScalarGridSpec(
+            num_scalar_prefetch=1,
+            grid=(requests,),
+            in_specs=in_specs,
+            out_specs=(
+                pl.BlockSpec((SUFFIX, cols), lambda r, s: (r, block)),
+                pl.BlockSpec((1, state_size, cols), lambda r, s: (r, 0, block)),
+            ),
+            scratch_shapes=[pltpu.VMEM((SUFFIX, cols), jnp.bfloat16)],
+        ),
         input_output_aliases=aliases,
         compiler_params=pltpu.CompilerParams(vmem_limit_bytes=48 * 1024 * 1024),
         cost_estimate=pl.CostEstimate(
@@ -158,7 +164,219 @@
             bytes_accessed=4 * cols * (tokens + requests * state_size),
             transcendentals=tokens * SUFFIX * heads,
         ),
-    )(chan, proj_bc, cum, cum_t, step_t, factor, grown, live, keep, gain, state, *carry)
+    )(places, chan, proj_bc, cum, cum_t, step_t, factor, grown, live, keep, gain, state, *carry)
+
+
+MESH = pl.DeviceIdType.MESH
+
+
+def flip(index, bits):
+    result = index
+    for bit in (1, 2, 4):
+        if bits & bit:
+            result = result + bit - 2 * bit * ((index // bit) % 2)
+    return result
+
+
+def project(tokens_vmem, w_ref, out_ref, total, tile):
+    depth, cols = w_ref.shape
+    rows = tokens_vmem.shape[0]
+    k_tile = min(depth, 2048)
+    steps = depth // k_tile
+
+    def step(w_block, out_block):
+        k = pl.program_id(1)
+        columns = pl.ds(pl.multiple_of(k * k_tile, k_tile), k_tile)
+        part = jnp.dot(
+            tokens_vmem[:, columns], w_block[...], preferred_element_type=jnp.float32
+        )
+
+        @pl.when(k == 0)
+        def _():
+            total[:, :tile] = part
+
+        @pl.when(k > 0)
+        def _():
+            total[:, :tile] += part
+
+        @pl.when(k == steps - 1)
+        def _():
+            out_block[...] = total[:, :tile].astype(out_block.dtype)
+
+    pltpu.emit_pipeline(
+        step,
+        grid=(cols // tile, steps),
+        in_specs=[pl.BlockSpec((k_tile, tile), lambda n, k: (k, n))],
+        out_specs=[pl.BlockSpec((rows, tile), lambda n, k: (0, n))],
+    )(w_ref, out_ref)
+
+
+def exchange_kernel(bc_cols, tile, tokens_ref, small_ref, x_ref, blocks_ref, chan_ref, proj_ref, dt_ref,
+                    w_small, w_all, landed, state_ref, tokens_vmem, total, w_send, w_recv, w_here,
+                    snap_send, snap_recv, z_send, z_recv, z_here, tokens_sem):
+    me, my_z = lax.axis_index("cache"), lax.axis_index("head")
+    n_cache, n_head = blocks_ref.shape[0], blocks_ref.shape[1]
+    depth = small_ref.shape[0]
+    half = depth // 2
+
+    barrier = pltpu.get_barrier_semaphore()
+    for a in range(1, n_cache):
+        pl.semaphore_signal(barrier, inc=1, device_id=(flip(me, a), my_z), device_id_type=MESH)
+    for b in range(1, n_head):
+        pl.semaphore_signal(barrier, inc=1, device_id=(me, flip(my_z, b)), device_id_type=MESH)
+    pl.semaphore_wait(barrier, n_cache + n_head - 2)
+
+    chunks = [(small_ref, w_small, 0, small_ref.shape[1])]
+    chunks += [(x_ref, w_all, c, tile) for c in range(0, x_ref.shape[1], tile)]
+
+    def remote(src, dst, sends, recvs, index, device):
+        return pltpu.make_async_remote_copy(
+            src_ref=src, dst_ref=dst, send_sem=sends.at[index], recv_sem=recvs.at[index],
+            device_id=device, device_id_type=MESH,
+        )
+
+    def weights(i, kind):
+        src, dst, first, width = chunks[i]
+        to, owner, low, rows = (
+            (2, 0, 0, depth), (4, 0, 0, depth), (1, 0, 0, depth),
+            (4, 2, 0, half), (1, 2, 0, depth), (2, 4, half, half), (1, 4, 0, depth),
+            (1, 6, 0, half), (1, 6, half, half),
+        )[kind]
+        columns = pl.ds(first, width)
+        place = dst.at[pl.ds(pl.multiple_of(flip(me, owner) * depth, depth) + low, rows), columns]
+        source = src.at[:, columns] if kind < 3 else place
+        return remote(source, place, w_send, w_recv, (i, kind), (flip(me, to), my_z))
+
+    def own(i):
+        src, dst, first, width = chunks[i]
+        columns = pl.ds(first, width)
+        rows = pl.ds(pl.multiple_of(me * depth, depth), depth)
+        return pltpu.make_async_copy(src.at[:, columns], dst.at[rows, columns], w_here.at[i])
+
+    def snapshot(a):
+        peer = flip(me, a)
+        return remote(blocks_ref.at[peer], landed.at[me], snap_send, snap_recv, (a - 1,), (peer, my_z))
+
+    def along_z(a, b):
+        peer = flip(me, a)
+        to = flip(my_z, b)
+        src = (landed if a else blocks_ref).at[peer, to]
+        if b == 0:
+            return pltpu.make_async_copy(src, state_ref.at[my_z, peer], z_here.at[a])
+        return remote(src, state_ref.at[my_z, peer], z_send, z_recv, (a, b - 1), (me, to))
+
+    count = len(chunks)
+    tokens_copy = pltpu.make_async_copy(tokens_ref, tokens_vmem, tokens_sem)
+
+    def start_direct(i):
+        for kind in range(3):
+            weights(i, kind).start()
+        own(i).start()
+
+    def arrive_direct(i):
+        weights(i, 0).wait_recv()
+        weights(i, 3).start()
+        weights(i, 4).start()
+        weights(i, 1).wait_recv()
+        weights(i, 5).start()
+        weights(i, 6).start()
+
+    def arrive_diagonal(i):
+        weights(i, 3).wait_recv()
+        weights(i, 7).start()
+        weights(i, 5).wait_recv()
+        weights(i, 8).start()
+
+    def arrive_rest(i):
+        own(i).wait()
+        for kind in (2, 4, 6, 7, 8):
+            weights(i, kind).wait_recv()
+
+    def multiply(i):
+        if i == 0:
+            project(tokens_vmem, w_small.at[:, :bc_cols], proj_ref, total, min(tile, bc_cols))
+            project(tokens_vmem, w_small.at[:, bc_cols:], dt_ref, total, LANES)
+        else:
+            columns = pl.ds(chunks[i][2], tile)
+            project(tokens_vmem, w_all.at[:, columns], chan_ref.at[:, columns], total, tile)
+
+    for b in (1, 2, 3, 0):
+        along_z(0, b).start()
+    for a in (1, 2, 4, 3, 5, 6, 7):
+        snapshot(a).start()
+    start_direct(0)
+    tokens_copy.start()
+    start_direct(1)
+    for a in (1, 2, 4, 3, 5, 6, 7):
+        snapshot(a).wait_recv()
+        for b in (1, 2, 3, 0):
+            along_z(a, b).start()
+    tokens_copy.wait()
+    for i in range(count + 1):
+        if i < count:
+            arrive_direct(i)
+            if i + 2 < count:
+                start_direct(i + 2)
+        if i >= 1:
+            arrive_diagonal(i - 1)
+            arrive_rest(i - 1)
+            multiply(i - 1)
+    for a in range(n_cache):
+        along_z(a, 0).wait()
+        for b in range(1, n_head):
+            along_z(a, b).wait()
+    for a in range(1, n_cache):
+        snapshot(a).wait_send()
+    for i in range(count):
+        for kind in range(9):
+            weights(i, kind).wait_send()
+
+
+def exchange(tokens, local_small, w_x, blocks, bc_cols):
+    rows, model = tokens.shape
+    n_cache, n_head, state_rows, width = blocks.shape
+    small_cols, cols = local_small.shape[1], w_x.shape[1]
+    tile = 512
+    count = 1 + cols // tile
+    bf16 = jnp.bfloat16
+    anywhere = pl.BlockSpec(memory_space=pl.ANY)
+    dma = pltpu.SemaphoreType.DMA
+    outs = pl.pallas_call(
+        functools.partial(exchange_kernel, bc_cols, tile),
+        out_shape=(
+            jax.ShapeDtypeStruct((rows, cols), bf16),
+            jax.ShapeDtypeStruct((rows, bc_cols), bf16),
+            jax.ShapeDtypeStruct((rows, small_cols - bc_cols), jnp.float32),
+            jax.ShapeDtypeStruct((model, small_cols), bf16),
+            jax.ShapeDtypeStruct((model, cols), bf16),
+            jax.ShapeDtypeStruct(blocks.shape, bf16),
+            jax.ShapeDtypeStruct((n_head, n_cache, state_rows, width), bf16),
+        ),
+        in_specs=[anywhere] * 4,
+        out_specs=[anywhere] * 7,
+        scratch_shapes=[
+            pltpu.VMEM(tokens.shape, bf16),
+            pltpu.VMEM((rows, tile), jnp.float32),
+            dma((count, 9)),
+            dma((count, 9)),
+            dma((count,)),
+            dma((n_cache - 1,)),
+            dma((n_cache - 1,)),
+            dma((n_cache, n_head - 1)),
+            dma((n_cache, n_head - 1)),
+            dma((n_cache,)),
+            dma,
+        ],
+        compiler_params=pltpu.CompilerParams(
+            collective_id=0, has_side_effects=True, vmem_limit_bytes=48 * 1024 * 1024
+        ),
+        cost_estimate=pl.CostEstimate(
+            flops=2 * rows * model * (cols + small_cols),
+            bytes_accessed=4 * model * (cols + small_cols),
+            transcendentals=0,
+        ),
+    )(tokens, local_small, w_x, blocks)
+    return outs[0], outs[1], outs[2], outs[6]
 
 
 def body(tokens, w_x, w_bc, w_dt, dt_bias, decay_log, skip_gain, pool, owners, slots, offsets):
@@ -174,33 +392,45 @@
     head_count = lax.axis_size("head")
     my_cache = lax.axis_index("cache")
 
+    one_kernel = cache_count == 8 and head_count == 4
     chunks = []
     for group in range(groups_here):
-        pieces = 2 if group == groups_here - 1 else 1
+        pieces = 2 if group == groups_here - 1 and not one_kernel else 1
         size = per_group // pieces
         chunks += [(group * per_group + i * size, size, group) for i in range(pieces)]
 
-    local_small = jnp.concatenate([w_bc.reshape(w_bc.shape[0], bc_cols), w_dt], axis=1)
-    w_small = lax.all_gather(local_small, "cache", axis=0, tiled=True)
-    w_parts = [
-        lax.all_gather(
-            w_x[:, first * head_width : (first + size) * head_width], "cache", axis=0, tiled=True
-        )
-        for first, size, _ in chunks
-    ]
-
+    pad = -w_dt.shape[1] % LANES
+    local_small = jnp.concatenate(
+        [w_bc.reshape(w_bc.shape[0], bc_cols), jnp.pad(w_dt, ((0, 0), (0, pad)))], axis=1
+    )
     owner_table = owners[:, 0].reshape(cache_count, requests_here)
     slot_table = slots[:, 0].reshape(cache_count, requests_here)
     chosen_slot = jnp.sum(jnp.where(owner_table == my_cache, slot_table, 0), axis=1)
     my_owners = lax.dynamic_slice_in_dim(owners[:, 0], my_cache * requests_here, requests_here)
     blocks = pick_for_owners(pool, chosen_slot, head_count)
-    received = lax.all_to_all(blocks, "cache", split_axis=0, concat_axis=0, tiled=True)
-    wanted = pick_for_requests(received, my_owners)
-    state = lax.all_to_all(wanted, "head", split_axis=0, concat_axis=0, tiled=True)
-
-    part_small = jnp.dot(tokens, w_small, preferred_element_type=jnp.float32)
-    proj_bc = part_small[:, :bc_cols].astype(jnp.bfloat16)
-    dt_raw = part_small[:, bc_cols:].reshape(requests_here, SUFFIX, heads_here)
+
+    if one_kernel:
+        chan_all, proj_bc, part_dt, state = exchange(tokens, local_small, w_x, blocks, bc_cols)
+        places = my_owners
+    else:
+        w_small = lax.all_gather(local_small, "cache", axis=0, tiled=True)
+        w_parts = [
+            lax.all_gather(
+                w_x[:, first * head_width : (first + size) * head_width],
+                "cache",
+                axis=0,
+                tiled=True,
+            )
+            for first, size, _ in chunks
+        ]
+        received = lax.all_to_all(blocks, "cache", split_axis=0, concat_axis=0, tiled=True)
+        wanted = pick_for_requests(received, my_owners)
+        state = lax.all_to_all(wanted, "head", split_axis=0, concat_axis=0, tiled=True)
+        places = jnp.arange(requests_here, dtype=jnp.int32)
+        part_small = jnp.dot(tokens, w_small, preferred_element_type=jnp.float32)
+        proj_bc = part_small[:, :bc_cols].astype(jnp.bfloat16)
+        part_dt = part_small[:, bc_cols:]
+    dt_raw = part_dt[:, :heads_here].reshape(requests_here, SUFFIX, heads_here)
     positions = jnp.arange(SUFFIX, dtype=jnp.int32)
     live = (positions[None, :] >= offsets[:, None]).astype(jnp.float32)
     step = jax.nn.softplus(dt_raw + dt_bias[None, None, :]) * live[:, :, None]
@@ -220,9 +450,15 @@
     )
 
     carry = ()
-    for (first, size, group), w_part in zip(chunks, w_parts):
-        chan = jnp.dot(tokens, w_part, preferred_element_type=jnp.float32).astype(jnp.bfloat16)
-        carry = ssd(first, size, group, chan, proj_bc, small, state, carry, total_cols)
+    for place, (first, size, group) in enumerate(chunks):
+        if one_kernel:
+            chan = chan_all
+        else:
+            chan = jnp.dot(tokens, w_parts[place], preferred_element_type=jnp.float32)
+            chan = chan.astype(jnp.bfloat16)
+        carry = ssd(
+            first, size, group, chan, proj_bc, small, state, places, carry, total_cols
+        )
     return tuple(carry)
 
 

time: 437 us -> 364 us (0.83)
  Pallas kernels: 41.5 us -> 356 us
  waiting for transfers between devices: 284 us -> 0 us
  matrix products: 67.5 us -> 0 us
  between operations: 14 us -> 0.79 us
  starting transfers between devices: 11.9 us -> 0 us
  local copies, waits for them, and re-layouts: 12 us -> 3.54 us
    pallas_call x1, Pallas kernels: 7.57 us -> 326 us  [exchange(): pl.pallas_call(functools.partial(exchange_kernel, bc_cols, tile), out_sha...]
    all_gather x4 -> x0, waiting for transfers between devices: 154 us -> none  [the longest x1 81.1 us: body(): w_small = lax.all_gather(local_small, 'cache', axis=0, tiled=True)]
    all_to_all x2 -> x0, waiting for transfers between devices: 130 us -> none  [the longest x1 130 us: body(): lax.all_to_all(blocks, 'cache', split_axis=0, concat_axis=0, tiled=True)]
    dot_general x4 -> x0, matrix products: 67.5 us -> none  [the longest x3 46.9 us: body(): jnp.dot(tokens, w_part, preferred_element_type=jnp.float32)]
    all_to_all x2 -> x0, starting transfers between devices: 11.7 us -> none  [the longest x1 6.22 us: body(): lax.all_to_all(wanted, 'head', split_axis=0, concat_axis=0, tiled=True)]
    slice x4 -> x0, local copies, waits for them, and re-layouts: 6.5 us -> none  [the longest x2 6.23 us: body(): w_x[:, first * head_width:(first + size) * head_width]]
    pallas_call x3 -> x2, Pallas kernels: 24.1 us -> 20.4 us  [ssd(): pl.pallas_call(functools.partial(ssd_kernel, first, heads, width, len(car...]
  transfers between devices with their start and end apart: 6 -> 0, of which waited for: 3 -> 0; matrix products, arithmetic and copies ran while one was open for 18% -> 0% of each run, Pallas kernels for 4% -> 0%
where the time goes in v2:
time: 364 us; the launch traced here: 363 us
  Pallas kernels  356 us (98%)
    pallas_call x1, Pallas kernels, exchange(): pl.pallas_call(functools.partial(exchange_kernel, bc_cols, tile), out_sha...  326 us
    pallas_call x2, Pallas kernels, ssd(): pl.pallas_call(functools.partial(ssd_kernel, first, heads, width, len(car...  20.4 us
    pallas_call x1, Pallas kernels, pick_for_owners(): pl.pallas_call(pick_kernel, out_shape=jax.ShapeDtypeStruct((count, parts,...  9.64 us

profile of v2, /device:TPU:0, one launch (start us, length us, event | category | flops | bytes accessed | tf_op | source)
XLA Modules:
  0.0 362.7 jit_solution(10456670565306901596)
XLA Ops:
  0.6 0.7 fusion.10
  1.3 0.1 select_n.23
  1.4 0.6 reduce_sum.9.index_ref
  2.0 9.6 %shard_map.122.blocks_ref = bf16[8,4,64,2048]{3,2,1,0:T(8,128)(2,1)} custom-call(s32[8]{0:T(128)} %reduce_sum.9.index_ref, bf16[8,64,8192]{2,1,0:T(8,128)(2,1)} %src_ref.1), custom_call_target="tpu_custom_call" | custom-call | bytes 16777216 | tf_op jit(solution)/shard_map/pallas_call | solution.py:25
  11.7 2.2 copy.27
  13.9 0.2 copy.19
  14.1 0.2 fusion.1.small_ref
  14.3 0.0 copy-start.5
  14.3 325.9 %shard_map.123 = (bf16[768,2048]{1,0:T(8,128)(2,1)}, bf16[768,1024]{1,0:T(8,128)(2,1)S(1)}, f32[768,128]{1,0:T(8,128)S(1)}, bf16[8192,1152]{1,0:T(8,128)(2,1)}, ...) custom-call(bf16[768,8192]{1,0:T(8,128)(2,1)} %tokens_ref.1, ...), custom_call_target="tpu_custom_call" | custom-call | flops 40265318400 | bytes 104857600 | tf_op jit(solution)/shard_map/pallas_call | solution.py:344
  340.2 0.1 copy.20
  340.3 0.1 fusion.8
  340.4 0.1 fusion.6
  340.6 0.2 copy.21
  340.8 0.4 reduce_window_sum.11
  341.2 0.3 bitcast_exponential_fusion
  341.5 0.1 broadcast_in_dim.18
  341.6 0.1 broadcast_in_dim.19.refs_8_
  341.7 0.1 copy.22
  341.8 0.1 dynamic-slice_bitcast_fusion.index_ref
  341.9 0.2 copy.29
  342.1 0.1 broadcast_in_dim.20
  342.2 0.1 broadcast_in_dim_reshape.3.refs_9_
  342.3 10.2 %shard_map.124 = (bf16[768,2048]{1,0:T(8,128)(2,1)}, bf16[6,256,2048]{2,1,0:T(8,128)(2,1)}) custom-call(s32[6]{0:T(128)S(1)} %dynamic-slice_bitcast_fusion.index_ref, bf16[768,2048]{1,0:T(8,128)(2,1)} %get-tuple-element.8.refs_0_, bf16[768,1024]{1,0:T(8,128)(2,1)S(1)} %get-tuple-element.9.refs_1_, f32[768,32]{1,0:T(8,128)S(1)} %bitcast.31, ...), custom_call_target="tpu_custom_call" | custom-call | flops 1207959552 | bytes 9437184 | tf_op jit(solution)/shard_map/pallas_call | solution.py:144
  352.5 10.2 %shard_map.125 = (bf16[768,2048]{1,0:T(8,128)(2,1)}, bf16[6,256,2048]{2,1,0:T(8,128)(2,1)}) custom-call(s32[6]{0:T(128)S(1)} %dynamic-slice_bitcast_fusion.index_ref, bf16[768,2048]{1,0:T(8,128)(2,1)} %get-tuple-element.8.refs_0_, bf16[768,1024]{1,0:T(8,128)(2,1)S(1)} %get-tuple-element.9.refs_1_, ...), custom_call_target="tpu_custom_call", output_to_operand_aliasing={{0}: (12, {}), {1}: (13, {})} | custom-call | flops 1207959552 | bytes 9437184 | tf_op jit(solution)/shard_map/pallas_call | solution.py:144
  (15 shorter events, 0.1 us)
Async XLA Ops:
  11.7 2.2 copy-start
  14.3 326.1 %copy-start.2 = (s32[6]{0:T(128)S(1)}, s32[6]{0:T(128)}, u32[]{:S(2)}) copy-start(s32[6]{0:T(128)} %param.21) | copy-start | bytes 76
  14.3 326.1 %copy-start.5 = (f32[32]{0:T(128)S(1)}, f32[32]{0:T(128)}, u32[]{:S(2)}) copy-start(f32[32]{0:T(128)} %param.16) | copy-start | bytes 388
  14.3 326.1 %copy-start.1 = (f32[32]{0:T(128)S(1)}, f32[32]{0:T(128)}, u32[]{:S(2)}) copy-start(f32[32]{0:T(128)} %param.15) | copy-start | bytes 388
  340.2 1.7 copy-start.4
  340.2 1.9 copy-start.3

commit v3 on v2

--- a/solution.py
+++ b/solution.py
@@ -211,14 +211,16 @@
     )(w_ref, out_ref)
 
 
-def exchange_kernel(bc_cols, tile, tokens_ref, small_ref, x_ref, blocks_ref, chan_ref, proj_ref, dt_ref,
-                    w_small, w_all, landed, state_ref, tokens_vmem, total, w_send, w_recv, w_here,
-                    snap_send, snap_recv, z_send, z_recv, z_here, tokens_sem):
+def exchange_kernel(bc_cols, tile, slots_ref, tokens_ref, small_ref, x_ref, pool_ref, chan_ref, proj_ref, dt_ref,
+                    w_small, w_all, landed, state_ref, tokens_vmem, pool_vmem, picked, stage_x, stage_small, stage_z, total, w_send, w_recv, w_here,
+                    snap_send, snap_recv, z_send, z_recv, z_here, local_sem):
     me, my_z = lax.axis_index("cache"), lax.axis_index("head")
-    n_cache, n_head = blocks_ref.shape[0], blocks_ref.shape[1]
+    n_cache, n_head, width = picked.shape[0], picked.shape[1], picked.shape[3]
     depth = small_ref.shape[0]
     half = depth // 2
 
+    pool_copy = pltpu.make_async_copy(pool_ref, pool_vmem, local_sem.at[0])
+    pool_copy.start()
     barrier = pltpu.get_barrier_semaphore()
     for a in range(1, n_cache):
         pl.semaphore_signal(barrier, inc=1, device_id=(flip(me, a), my_z), device_id_type=MESH)
@@ -226,8 +228,10 @@
         pl.semaphore_signal(barrier, inc=1, device_id=(me, flip(my_z, b)), device_id_type=MESH)
     pl.semaphore_wait(barrier, n_cache + n_head - 2)
 
-    chunks = [(small_ref, w_small, 0, small_ref.shape[1])]
-    chunks += [(x_ref, w_all, c, tile) for c in range(0, x_ref.shape[1], tile)]
+    chunks = [(x_ref, w_all, c, tile) for c in range(0, x_ref.shape[1] - tile, tile)]
+    for c in range(x_ref.shape[1] - tile, x_ref.shape[1], tile // 2):
+        chunks.append((x_ref, w_all, c, tile // 2))
+    chunks.insert(1, (small_ref, w_small, 0, small_ref.shape[1]))
 
     def remote(src, dst, sends, recvs, index, device):
         return pltpu.make_async_remote_copy(
@@ -247,31 +251,47 @@
         source = src.at[:, columns] if kind < 3 else place
         return remote(source, place, w_send, w_recv, (i, kind), (flip(me, to), my_z))
 
-    def own(i):
+    def own_in(i):
+        src, _, first, width = chunks[i]
+        columns = pl.ds(first, width)
+        stage = stage_small if src is small_ref else stage_x
+        return pltpu.make_async_copy(src.at[:, columns], stage.at[:, columns], w_here.at[0, i])
+
+    def own_out(i):
         src, dst, first, width = chunks[i]
         columns = pl.ds(first, width)
+        stage = stage_small if src is small_ref else stage_x
         rows = pl.ds(pl.multiple_of(me * depth, depth), depth)
-        return pltpu.make_async_copy(src.at[:, columns], dst.at[rows, columns], w_here.at[i])
+        return pltpu.make_async_copy(stage.at[:, columns], dst.at[rows, columns], w_here.at[1, i])
 
     def snapshot(a):
         peer = flip(me, a)
-        return remote(blocks_ref.at[peer], landed.at[me], snap_send, snap_recv, (a - 1,), (peer, my_z))
+        return remote(picked.at[peer], landed.at[me], snap_send, snap_recv, (a - 1,), (peer, my_z))
 
     def along_z(a, b):
         peer = flip(me, a)
         to = flip(my_z, b)
-        src = (landed if a else blocks_ref).at[peer, to]
-        if b == 0:
-            return pltpu.make_async_copy(src, state_ref.at[my_z, peer], z_here.at[a])
+        src = (landed if a else picked).at[peer, to]
         return remote(src, state_ref.at[my_z, peer], z_send, z_recv, (a, b - 1), (me, to))
 
+    def stay_in(a):
+        return pltpu.make_async_copy(
+            landed.at[flip(me, a), my_z], stage_z.at[a - 1], z_here.at[0, a]
+        )
+
+    def stay_out(a):
+        peer = flip(me, a)
+        src = stage_z.at[a - 1] if a else picked.at[peer, my_z]
+        return pltpu.make_async_copy(src, state_ref.at[my_z, peer], z_here.at[1, a])
+
     count = len(chunks)
-    tokens_copy = pltpu.make_async_copy(tokens_ref, tokens_vmem, tokens_sem)
+    tokens_copy = pltpu.make_async_copy(tokens_ref, tokens_vmem, local_sem.at[1])
 
     def start_direct(i):
         for kind in range(3):
             weights(i, kind).start()
-        own(i).start()
+        own_in(i).wait()
+        own_out(i).start()
 
     def arrive_direct(i):
         weights(i, 0).wait_recv()
@@ -288,41 +308,65 @@
         weights(i, 8).start()
 
     def arrive_rest(i):
-        own(i).wait()
+        own_out(i).wait()
         for kind in (2, 4, 6, 7, 8):
             weights(i, kind).wait_recv()
 
     def multiply(i):
-        if i == 0:
+        if chunks[i][0] is small_ref:
             project(tokens_vmem, w_small.at[:, :bc_cols], proj_ref, total, min(tile, bc_cols))
             project(tokens_vmem, w_small.at[:, bc_cols:], dt_ref, total, LANES)
         else:
-            columns = pl.ds(chunks[i][2], tile)
-            project(tokens_vmem, w_all.at[:, columns], chan_ref.at[:, columns], total, tile)
-
-    for b in (1, 2, 3, 0):
+            columns = pl.ds(chunks[i][2], chunks[i][3])
+            project(tokens_vmem, w_all.at[:, columns], chan_ref.at[:, columns], total, chunks[i][3])
+
+    def pass_on(a):
+        snapshot(a).wait_recv()
+        for b in (2, 3, 1):
+            along_z(a, b).start()
+        stay_in(a).start()
+
+    def pick(i, _):
+        slot = slots_ref[i]
+        for part in range(n_head):
+            picked[i, part] = pool_vmem[slot, :, part * width : (part + 1) * width]
+        return 0
+
+    for i in range(count):
+        own_in(i).start()
+    start_direct(0)
+    pool_copy.wait()
+    lax.fori_loop(0, n_cache, pick, 0)
+    for a in (6, 2, 4, 7, 3, 5, 1):
+        snapshot(a).start()
+    for b in (2, 3, 1):
         along_z(0, b).start()
-    for a in (1, 2, 4, 3, 5, 6, 7):
-        snapshot(a).start()
-    start_direct(0)
+    stay_out(0).start()
     tokens_copy.start()
+    pass_on(1)
+    pass_on(2)
+    pass_on(4)
     start_direct(1)
-    for a in (1, 2, 4, 3, 5, 6, 7):
-        snapshot(a).wait_recv()
-        for b in (1, 2, 3, 0):
-            along_z(a, b).start()
+    for a in (3, 5, 6, 7):
+        pass_on(a)
     tokens_copy.wait()
+    for a in range(1, n_cache):
+        stay_in(a).wait()
+        stay_out(a).start()
     for i in range(count + 1):
         if i < count:
             arrive_direct(i)
             if i + 2 < count:
                 start_direct(i + 2)
         if i >= 1:
-            arrive_diagonal(i - 1)
+            if i < count:
+                arrive_diagonal(i - 1)
             arrive_rest(i - 1)
+            if i == count - 1:
+                arrive_diagonal(i)
             multiply(i - 1)
     for a in range(n_cache):
-        along_z(a, 0).wait()
+        stay_out(a).wait()
         for b in range(1, n_head):
             along_z(a, b).wait()
     for a in range(1, n_cache):
@@ -332,12 +376,13 @@
             weights(i, kind).wait_send()
 
 
-def exchange(tokens, local_small, w_x, blocks, bc_cols):
+def exchange(chosen, tokens, local_small, w_x, pool, n_cache, n_head, bc_cols):
     rows, model = tokens.shape
-    n_cache, n_head, state_rows, width = blocks.shape
+    _, state_rows, width = pool.shape
+    width = width // n_head
     small_cols, cols = local_small.shape[1], w_x.shape[1]
     tile = 512
-    count = 1 + cols // tile
+    count = 2 + cols // tile
     bf16 = jnp.bfloat16
     anywhere = pl.BlockSpec(memory_space=pl.ANY)
     dma = pltpu.SemaphoreType.DMA
@@ -349,33 +394,38 @@
             jax.ShapeDtypeStruct((rows, small_cols - bc_cols), jnp.float32),
             jax.ShapeDtypeStruct((model, small_cols), bf16),
             jax.ShapeDtypeStruct((model, cols), bf16),
-            jax.ShapeDtypeStruct(blocks.shape, bf16),
+            jax.ShapeDtypeStruct((n_cache, n_head, state_rows, width), bf16),
             jax.ShapeDtypeStruct((n_head, n_cache, state_rows, width), bf16),
         ),
-        in_specs=[anywhere] * 4,
+        in_specs=[pl.BlockSpec(memory_space=pltpu.SMEM)] + [anywhere] * 4,
         out_specs=[anywhere] * 7,
         scratch_shapes=[
             pltpu.VMEM(tokens.shape, bf16),
+            pltpu.VMEM(pool.shape, bf16),
+            pltpu.VMEM((n_cache, n_head, state_rows, width), bf16),
+            pltpu.VMEM(w_x.shape, bf16),
+            pltpu.VMEM(local_small.shape, bf16),
+            pltpu.VMEM((n_cache - 1, state_rows, width), bf16),
             pltpu.VMEM((rows, tile), jnp.float32),
             dma((count, 9)),
             dma((count, 9)),
-            dma((count,)),
+            dma((2, count)),
             dma((n_cache - 1,)),
             dma((n_cache - 1,)),
             dma((n_cache, n_head - 1)),
             dma((n_cache, n_head - 1)),
-            dma((n_cache,)),
-            dma,
+            dma((2, n_cache)),
+            dma((2,)),
         ],
         compiler_params=pltpu.CompilerParams(
-            collective_id=0, has_side_effects=True, vmem_limit_bytes=48 * 1024 * 1024
+            collective_id=0, has_side_effects=True, vmem_limit_bytes=56 * 1024 * 1024
         ),
         cost_estimate=pl.CostEstimate(
             flops=2 * rows * model * (cols + small_cols),
             bytes_accessed=4 * model * (cols + small_cols),
             transcendentals=0,
         ),
-    )(tokens, local_small, w_x, blocks)
+    )(chosen, tokens, local_small, w_x, pool)
     return outs[0], outs[1], outs[2], outs[6]
 
 
@@ -407,10 +457,11 @@
     slot_table = slots[:, 0].reshape(cache_count, requests_here)
     chosen_slot = jnp.sum(jnp.where(owner_table == my_cache, slot_table, 0), axis=1)
     my_owners = lax.dynamic_slice_in_dim(owners[:, 0], my_cache * requests_here, requests_here)
-    blocks = pick_for_owners(pool, chosen_slot, head_count)
 
     if one_kernel:
-        chan_all, proj_bc, part_dt, state = exchange(tokens, local_small, w_x, blocks, bc_cols)
+        chan_all, proj_bc, part_dt, state = exchange(
+            chosen_slot, tokens, local_small, w_x, pool, cache_count, head_count, bc_cols
+        )
         places = my_owners
     else:
         w_small = lax.all_gather(local_small, "cache", axis=0, tiled=True)
@@ -423,6 +474,7 @@
             )
             for first, size, _ in chunks
         ]
+        blocks = pick_for_owners(pool, chosen_slot, head_count)
         received = lax.all_to_all(blocks, "cache", split_axis=0, concat_axis=0, tiled=True)
         wanted = pick_for_requests(received, my_owners)
         state = lax.all_to_all(wanted, "head", split_axis=0, concat_axis=0, tiled=True)

time: 364 us -> 356 us (0.978)
  Pallas kernels: 356 us -> 344 us
    pallas_call x1 -> x0, Pallas kernels: 9.64 us -> none  [pick_for_owners(): pl.pallas_call(pick_kernel, out_shape=jax.ShapeDtypeStruct((count, parts,...]
where the time goes in v3:
time: 356 us; the launch traced here: 355 us
  Pallas kernels  344 us (97%)
  other arithmetic  4.93 us (1%)
  local copies, waits for them, and re-layouts  4.61 us (1%)
    pallas_call x1, Pallas kernels, exchange(): pl.pallas_call(functools.partial(exchange_kernel, bc_cols, tile), out_sha...  324 us
    pallas_call x2, Pallas kernels, ssd(): pl.pallas_call(functools.partial(ssd_kernel, first, heads, width, len(car...  20.4 us

profile of v3, /device:TPU:0, one launch (start us, length us, event | category | flops | bytes accessed | tf_op | source)
XLA Modules:
  0.0 354.7 jit_solution(14078114180039357370)
XLA Ops:
  0.6 0.7 fusion.10
  1.4 0.1 select_n.23
  1.4 0.6 reduce_sum.9.slots_ref
  2.1 2.1 copy.27
  4.2 0.2 copy.19
  4.4 1.6 fusion.1.small_ref
  6.0 324.0 %shard_map.122 = (bf16[768,2048]{1,0:T(8,128)(2,1)}, bf16[768,1024]{1,0:T(8,128)(2,1)}, f32[768,128]{1,0:T(8,128)}, bf16[8192,1152]{1,0:T(8,128)(2,1)}, bf16[819...) custom-call(s32[8]{0:T(128)} %reduce_sum.9.slots_ref, ...), custom_call_target="tpu_custom_call" | custom-call | flops 40265318400 | bytes 104857600 | tf_op jit(solution)/shard_map/pallas_call | solution.py:389
  330.0 0.0 copy-start.5
  330.0 0.0 copy-start.4
  330.1 1.2 copy.20
  331.3 0.1 fusion.8
  331.4 0.1 fusion.6
  331.5 0.2 copy.21
  331.7 0.4 reduce_window_sum.11
  332.1 1.4 bitcast_exponential_fusion
  333.5 0.1 broadcast_in_dim.18
  333.6 0.1 broadcast_in_dim.19.refs_8_
  333.7 0.1 copy.22
  333.8 0.1 dynamic-slice_bitcast_fusion.index_ref
  333.9 0.2 copy.29
  334.1 0.1 broadcast_in_dim.20
  334.2 0.1 broadcast_in_dim_reshape.3.refs_9_
  334.3 10.2 %shard_map.123 = (bf16[768,2048]{1,0:T(8,128)(2,1)}, bf16[6,256,2048]{2,1,0:T(8,128)(2,1)}) custom-call(s32[6]{0:T(128)S(1)} %dynamic-slice_bitcast_fusion.index_ref, bf16[768,2048]{1,0:T(8,128)(2,1)} %get-tuple-element.8.refs_0_, bf16[768,1024]{1,0:T(8,128)(2,1)S(1)} %copy-done, f32[768,32]{1,0:T(8,128)S(1)} %bitcast.31, f32[6,32,128]{2,1,0:T(8,128)S(1)} %bitcast.35, ...), custom_call_target="tpu_custom_call" | custom-call | flops 1207959552 | bytes 9437184 | tf_op jit(solution)/shard_map/pallas_call | solution.py:144
  344.5 10.2 %shard_map.124 = (bf16[768,2048]{1,0:T(8,128)(2,1)}, bf16[6,256,2048]{2,1,0:T(8,128)(2,1)}) custom-call(s32[6]{0:T(128)S(1)} %dynamic-slice_bitcast_fusion.index_ref, bf16[768,2048]{1,0:T(8,128)(2,1)} %get-tuple-element.8.refs_0_, bf16[768,1024]{1,0:T(8,128)(2,1)S(1)} %copy-done, ...), custom_call_target="tpu_custom_call", output_to_operand_aliasing={{0}: (12, {}), {1}: (13, {})} | custom-call | flops 1207959552 | bytes 9437184 | tf_op jit(solution)/shard_map/pallas_call | solution.py:144
  (16 shorter events, 0.0 us)
Async XLA Ops:
  0.6 3.6 %copy-start.1 = (bf16[1024,32]{0,1:T(8,128)(2,1)S(1)}, bf16[1024,32]{0,1:T(8,128)(2,1)}, u32[]{:S(2)}) copy-start(bf16[1024,32]{0,1:T(8,128)(2,1)} %param.14) | copy-start | bytes 196612
  6.0 325.3 %copy-start.3 = (s32[6]{0:T(128)S(1)}, s32[6]{0:T(128)}, u32[]{:S(2)}) copy-start(s32[6]{0:T(128)} %param.21) | copy-start | bytes 76
  6.0 325.3 %copy-start.6 = (f32[32]{0:T(128)S(1)}, f32[32]{0:T(128)}, u32[]{:S(2)}) copy-start(f32[32]{0:T(128)} %param.16) | copy-start | bytes 388
  6.0 325.4 %copy-start.2 = (f32[32]{0:T(128)S(1)}, f32[32]{0:T(128)}, u32[]{:S(2)}) copy-start(f32[32]{0:T(128)} %param.15) | copy-start | bytes 388
  330.0 3.8 %copy-start.5 = (s32[48,1]{0,1:T(1,128)S(1)}, s32[48,1]{0,1:T(1,128)}, u32[]{:S(2)}) copy-start(s32[48,1]{0,1:T(1,128)} %param.19) | copy-start | bytes 580
  330.0 4.1 %copy-start.4 = (f32[32]{0:T(128)S(1)}, f32[32]{0:T(128)}, u32[]{:S(2)}) copy-start(f32[32]{0:T(128)} %param.17) | copy-start | bytes 388
  330.0 4.2 %copy-start = (bf16[768,1024]{1,0:T(8,128)(2,1)S(1)}, bf16[768,1024]{1,0:T(8,128)(2,1)}, u32[]{:S(2)}) copy-start(bf16[768,1024]{1,0:T(8,128)(2,1)} %get-tuple-element.9.refs_1_) | copy-start | bytes 4718596
